TPU v7x, 256 devices: a whole 4x4x8 slice. The times are simulated.
256 devices in a mesh: win: 8 (over y, z_lo), rcv: 32 (over x, z_hi, core).
Axes of the slice: x: 4, y: 4, z: 8 (z_hi: 4, z_lo: 2; z = z_hi * 2 + z_lo), core: 2. Of those that a mesh axis runs over, the one named last changes fastest.
Arguments:
- source_spectra: bfloat16 [256, 4096, 1024], P('win', 'rcv'), may hold values from -6 to 6
- receiver_spectra: bfloat16 [256, 512, 1024], P('win', 'rcv'), may hold values from -6 to 6
- source_block: int32 [1], replicated, may hold values from 0 to 31
- bad_channels: int32 [64], replicated, may hold values from 0 to 511
Outputs:
- correlations: float32 [128, 512, 1024], P('win', 'rcv')
Inputs may be any that keep to these rules, and one draw needn't show every extreme that they name: `source_block`: the rcv index of the device that holds the block. `bad_channels`: repeats may occur.
All inputs are finite; a program needn't handle non-finite values.
Results may differ from a plain program's by a relative error of at most 0.0036.
Values may be sent and summed in bfloat16 or wider, within the bound.
No kernel may reach another device: no remote copies, remote signals or barrier semaphores. Data moves between devices by JAX's collectives and lax.ppermute only.
A program may use at most 128 MiB of HBM per device.

v0:
```python
import math

import jax
import jax.numpy as jnp
from jax import lax
from jax.sharding import PartitionSpec as P


def broadcast(value, axis, source):
    kept = jnp.where(lax.axis_index(axis) == source, value, 0).astype(value.dtype)
    return lax.psum(kept, axis)


def whiten(spectra):
    half = spectra.shape[-1] // 2
    real_part = spectra[..., :half]
    imag_part = spectra[..., half:]
    power = real_part * real_part + imag_part * imag_part
    level = jnp.mean(power, axis=-1, keepdims=True)
    factor = lax.rsqrt(power + 0.1 * level + 1e-06)
    return jnp.concatenate([real_part * factor, imag_part * factor], axis=-1)


def inverse_table(lags, windows):
    half = lags // 2
    freq = jnp.arange(half, dtype=jnp.int32)[:, None]
    lag_index = jnp.arange(lags, dtype=jnp.int32)[None, :]
    phase = (freq * lag_index % lags).astype(jnp.float32) * (2.0 * math.pi / lags)
    weight = jnp.where(freq == 0, 1.0, 2.0).astype(jnp.float32) / jnp.sqrt(
        jnp.float32(windows * lags)
    )
    return jnp.concatenate([weight * jnp.cos(phase), -weight * jnp.sin(phase)], axis=0)


def to_lags(cross_rows, table):
    count, chans, width = cross_rows.shape
    flat = cross_rows.reshape(count * chans, width)
    result = jnp.dot(
        flat, table, precision=lax.Precision.HIGHEST, preferred_element_type=jnp.float32
    )
    return result.reshape(count, chans, table.shape[1])


def on_device(source_spectra, receiver_spectra, source_block, bad_channels):
    win_local, chans, lags = receiver_spectra.shape
    half = lags // 2
    own_white = whiten(source_spectra.astype(jnp.float32)).astype(jnp.bfloat16)
    src_white = broadcast(own_white, "rcv", source_block[0])
    channel_ids = lax.axis_index("rcv") * chans + jnp.arange(chans, dtype=jnp.int32)
    faulty = jnp.any(bad_channels[:, None] == channel_ids[None, :], axis=0)
    keep = jnp.where(faulty, 0.0, 1.0).astype(jnp.float32)
    rcv_white = (whiten(receiver_spectra.astype(jnp.float32)) * keep[None, :, None]).astype(
        jnp.bfloat16
    )
    s_re, s_im = (src_white[..., :half], src_white[..., half:])
    r_re, r_im = (rcv_white[..., :half], rcv_white[..., half:])
    cross_re = jnp.einsum(
        "wsf,wcf->scf", s_re, r_re, preferred_element_type=jnp.float32
    ) + jnp.einsum("wsf,wcf->scf", s_im, r_im, preferred_element_type=jnp.float32)
    cross_im = jnp.einsum(
        "wsf,wcf->scf", s_re, r_im, preferred_element_type=jnp.float32
    ) - jnp.einsum("wsf,wcf->scf", s_im, r_re, preferred_element_type=jnp.float32)
    cross = jnp.concatenate([cross_re, cross_im], axis=-1)
    table = inverse_table(lags, win_local * lax.axis_size("win"))
    return lax.psum_scatter(to_lags(cross, table), "win", scatter_dimension=0, tiled=True)


def solution(mesh):
    in_specs = (P("win", "rcv", None), P("win", "rcv", None), P(), P())
    out_specs = P("win", "rcv", None)
    return jax.shard_map(
        on_device, mesh=mesh, in_specs=in_specs, out_specs=out_specs, check_vma=False
    )
```

profile of v0, /device:TPU:1, one launch (start us, length us, event | category | flops | bytes accessed | tf_op | source)
XLA Modules:
  0.0 651.9 jit_solution(8966475779207950950)
XLA Ops:
  6.5 0.0 all-reduce.2.cloned.1.call-start
  6.5 11.3 %convert_element_type.19 = f32[32,128,1024]{2,1,0:T(8,128)} convert(bf16[32,128,1024]{2,1,0:T(8,128)(2,1)} %param.4) | non-fusion elementwise | flops 4194304 | bytes 25165824 | tf_op jit(solution)/shard_map/convert_element_type | solution.py:47
  17.8 0.0 copy-start
  17.8 6.6 %fusion.16 = f32[32,128]{1,0:T(8,128)S(1)} fusion(f32[32,128,1024]{2,1,0:T(8,128)} %convert_element_type.19), kind=kLoop, calls=%fused_computation.41 | loop fusion | flops 8384512 | bytes 16793600 | tf_op jit(solution)/shard_map/reduce_sum | solution.py:19
  24.5 4.0 copy-done
  28.4 4.5 multiply_convert_fusion.1
  33.6 7.7 %maximum_select_fusion = bf16[32,128,1024]{2,1,0:T(8,128)(2,1)} fusion(bf16[32,128,512]{2,1,0:T(8,128)(2,1)} %get-tuple-element.6, bf16[32,128,512]{2,1,0:T(8,128)(2,1)} %get-tuple-element.5, pred[]{:T(512)S(6)} %eq.37), kind=kLoop, calls=%fused_computation | loop fusion | flops 20971520 | bytes 16777216 | tf_op jit(solution)/shard_map/jit(_where)/select_n | solution.py:10
  41.4 0.0 copy-start.5
  41.4 0.0 copy-start.6
  41.4 0.0 all-reduce.2.cloned.1.call-update
  41.4 0.0 reduce-scatter.2.cloned.1.call-start
  41.5 1.1 copy-done.5
  42.6 0.2 convert_element_type.17
  42.9 0.0 copy-done.6
  42.9 0.2 compare_reduce_fusion
  43.1 0.2 fusion.15
  43.3 0.3 slice_multiply_fusion.1
  43.6 0.3 fusion.9
  43.9 0.1 fusion.18
  44.1 2.4 copy.10
  46.5 3.0 copy.7
  49.5 9.6 %sine_multiply_fusion = (f32[512,1024]{1,0:T(8,128)}, f32[512,1024]{1,0:T(8,128)}) fusion(f32[512]{0:T(512)S(1)} %fusion.13, f32[512]{0:T(512)S(1)} %select_multiply_fusion), kind=kLoop, calls=%fused_computation.22 | loop fusion | flops 8388608 | bytes 4198400 | tf_op jit(solution)/shard_map/mul | solution.py:32
  59.1 309.8 %all-reduce.2.cloned.1.call-done = bf16[32,128,1024]{2,1,0:T(8,128)(2,1)} async-done(((bf16[32,128,1024]{2,1,0:T(8,128)(2,1)}), bf16[32,128,1024]{2,1,0:T(8,128)(2,1)}) %all-reduce.2.cloned.1.call-update) | async-done | bytes 8388624 | tf_op jit(solution)/shard_map/psum | solution.py:11
  368.8 5.8 fusion.17
  374.7 7.9 %copy.11 = bf16[32,128,512]{1,0,2:T(8,128)(2,1)} copy(bf16[32,128,512]{2,1,0:T(8,128)(2,1)} %get-tuple-element.7) | data formatting | bytes 8388608 | tf_op jit(solution)/shard_map/slice | solution.py:55
  382.6 0.0 copy-start.2
  382.6 0.0 copy-start.3
  382.6 5.5 fusion.20
  388.1 0.0 copy-done.2
  388.1 0.0 copy-done.3
  388.1 3.2 fusion.22
  391.3 7.9 %copy.8 = bf16[32,128,512]{1,0,2:T(8,128)(2,1)} copy(bf16[32,128,512]{2,1,0:T(8,128)(2,1)} %get-tuple-element.8) | data formatting | bytes 8388608 | tf_op jit(solution)/shard_map/slice | solution.py:55
  399.2 0.0 copy-start.1
  399.2 6.1 fusion.19
  405.3 0.0 copy-done.1
  405.3 3.2 fusion.21
  408.5 5.2 copy.12
  413.7 5.3 copy.14
  419.0 5.3 copy.9
  424.3 5.3 copy.13
  429.6 0.0 copy-start.4
  429.6 10.2 %subtract_bitcast_fusion = (f32[128,16,512]{2,0,1:T(8,128)S(1)}, f32[128,16,512]{2,0,1:T(8,128)}) fusion(f32[512,16,128]{0,2,1:T(8,128)} %copy.13, f32[512,16,128]{0,2,1:T(8,128)} %copy.14, f32[512,16,128]{0,2,1:T(8,128)} %copy.9, f32[512,16,128]{0,2,1:T(8,128)} %copy.12), kind=kLoop, calls=%fused_computation.12 | loop fusion | flops 2097152 | bytes 25165824 | tf_op jit(solution)/shard_map/sub | solution.py:60
  439.9 0.0 copy-done.4
  439.9 32.1 %fusion = f32[128,16,1024]{2,0,1:T(8,128)} fusion(f32[128,16,512]{2,0,1:T(8,128)S(1)} %get-tuple-element.13, f32[128,16,512]{2,0,1:T(8,128)} %get-tuple-element.14, f32[512,1024]{1,0:T(8,128)S(1)} %copy-done.4, f32[512,1024]{1,0:T(8,128)} %get-tuple-element.16), kind=kOutput, calls=%fused_computation.1 | convolution fusion | flops 25772949504 | bytes 20971520 | tf_op jit(solution)/shard_map/dot_general | solution.py:38
  471.9 0.0 reduce-scatter.2.cloned.1.call-update
  471.9 170.3 %reduce-scatter.2.cloned.1.call-done = f32[16,16,1024]{2,0,1:T(8,128)} async-done(((f32[128,16,1024]{2,0,1:T(8,128)}), f32[16,16,1024]{2,0,1:T(8,128)}) %reduce-scatter.2.cloned.1.call-update) | async-done | bytes 1048592 | tf_op jit(solution)/shard_map/reduce_scatter | solution.py:65
  642.3 2.8 copy.6
  (6 shorter events, 0.0 us)
Async XLA Ops:
  6.5 362.3 %all-reduce.2.cloned.1.call-start = ((), (), s32[]{:S(2)}) async-start(), calls=%async_computation.1 | async-start | bytes 16777216 | tf_op jit(solution)/shard_map/psum | solution.py:11
  17.8 10.6 %copy-start = (f32[32,128,1024]{2,1,0:T(8,128)S(1)}, f32[32,128,1024]{2,1,0:T(8,128)}, u32[]{:S(2)}) copy-start(f32[32,128,1024]{2,1,0:T(8,128)} %convert_element_type.19) | copy-start | bytes 50331652
  41.4 1.2 copy-start.5
  41.4 1.5 copy-start.6
  41.4 600.8 %reduce-scatter.2.cloned.1.call-start = ((), (), s32[]{:S(2)}) async-start(), calls=%async_computation.2 | async-start | bytes 9437184 | tf_op jit(solution)/shard_map/reduce_scatter | solution.py:65
  382.6 5.5 copy-start.2
  382.6 5.5 copy-start.3
  399.2 6.1 copy-start.1
  429.6 10.2 %copy-start.4 = (f32[512,1024]{1,0:T(8,128)S(1)}, f32[512,1024]{1,0:T(8,128)}, u32[]{:S(2)}) copy-start(f32[512,1024]{1,0:T(8,128)} %get-tuple-element.15) | copy-start | bytes 6291460
Sparse Core Ops, SparseCore 0:
  41.5 327.2 all-reduce.1
  472.1 170.1 reduce-scatter.1
where the time goes:
time: 653 us; the launch traced here: 652 us
  waiting for transfers between devices  480 us (74%)
  local copies, waits for them, and re-layouts  56.2 us (9%)
  other arithmetic  51.3 us (8%)
  matrix products  50.1 us (8%)
  between operations  14.2 us (2%)
    psum x1, waiting for transfers between devices, broadcast(): return lax.psum(kept, axis)  310 us
    reduce_scatter x1, waiting for transfers between devices, on_device(): lax.psum_scatter(to_lags(cross, table), 'win', scatter_dimension=0, tiled...  170 us
    dot_general x1, matrix products, to_lags(): jnp.dot(flat, table, precision=lax.Precision.HIGHEST, preferred_element_t...  32.1 us
    slice x3, local copies, waits for them, and re-layouts, on_device(): s_re, s_im = (src_white[..., :half], src_white[..., half:])  21.6 us
  transfers between devices with their start and end apart: 2, of which 2 were waited for; matrix products, arithmetic and copies ran while one was open for 3% of the time, Pallas kernels for 0%

commit v1 on v0

v1 whole, which is shorter than its diff:
```python
import functools
import math

import jax
import jax.numpy as jnp
import numpy as np
from jax import lax
from jax.experimental import pallas as pl
from jax.experimental.pallas import tpu as pltpu
from jax.sharding import Mesh
from jax.sharding import PartitionSpec as P

AXES = ("y", "zl", "x", "zh", "core")
SIZES = (4, 2, 4, 4, 2)
LAGS = 1024
HALF = 512
WINDOWS = 256
VMEM = 48 * 1024 * 1024


def whiten_parts(re, im):
    power = re * re + im * im
    level = jnp.mean(power, axis=-1, keepdims=True)
    factor = lax.rsqrt(power + 0.1 * level + 1e-06)
    return re * factor, im * factor


def source_kernel(place, src_ref, *refs):
    outs, held = refs[:8], refs[8]
    core, x = place[0], place[1]
    block = src_ref.shape[0]
    data = src_ref[...].astype(jnp.float32)
    re, im = whiten_parts(data[..., :HALF], data[..., HALF:])
    for k in range(2):
        half_re = jnp.concatenate(
            [re[:, w * 16 + k * 8 : w * 16 + k * 8 + 8] for w in range(8)], axis=1
        )
        half_im = jnp.concatenate(
            [im[:, w * 16 + k * 8 : w * 16 + k * 8 + 8] for w in range(8)], axis=1
        )
        for q in range(4):
            lanes = slice(q * 128, q * 128 + 128)
            held[k * 4 + q, :, :, :128] = half_re[..., lanes].astype(jnp.bfloat16)
            held[k * 4 + q, :, :, 128:] = half_im[..., lanes].astype(jnp.bfloat16)
    for j in range(2):
        k = core if j == 0 else 1 - core
        for r in range(4):
            outs[j * 4 + r][...] = held[k * 4 + lax.rem(x + r, 4)]


def source_pieces(src, core, x):
    windows, sources, _ = src.shape
    block = 4
    place = jnp.stack([core, x]).astype(jnp.int32)
    piece = jax.ShapeDtypeStruct((windows, 64, 256), jnp.bfloat16)
    return pl.pallas_call(
        source_kernel,
        out_shape=[piece] * 8,
        grid_spec=pltpu.PrefetchScalarGridSpec(
            num_scalar_prefetch=1,
            grid=(windows // block,),
            in_specs=[pl.BlockSpec((block, sources, LAGS), lambda i, p: (i, 0, 0))],
            out_specs=[pl.BlockSpec((block, 64, 256), lambda i, p: (i, 0, 0))] * 8,
            scratch_shapes=[pltpu.VMEM((8, block, 64, 256), jnp.bfloat16)],
        ),
        compiler_params=pltpu.CompilerParams(vmem_limit_bytes=VMEM),
        cost_estimate=pl.CostEstimate(
            flops=40_000_000, bytes_accessed=16 * 2**20, transcendentals=2_000_000
        ),
    )(place, src)


def cross_kernel(src_ref, rcv_ref, out_ref, acc):
    lane = lax.broadcasted_iota(jnp.int32, (128, 128), 1)
    is_real = lax.rem(lane, 64) < 32
    first = lane < 64
    for win in range(8):
        plain = src_ref[win].astype(jnp.float32)
        turned = jnp.where(
            is_real, -pltpu.roll(plain, 96, axis=1), pltpu.roll(plain, 32, axis=1)
        )
        rows = jnp.concatenate(
            [
                jnp.where(first, plain, 0.0),
                jnp.where(first, turned, 0.0),
                jnp.where(first, 0.0, plain),
                jnp.where(first, 0.0, turned),
            ],
            axis=0,
        ).astype(jnp.bfloat16)
        part = lax.dot_general(
            rows, rcv_ref[win], (((1,), (1,)), ((), ())), preferred_element_type=jnp.float32
        )
        if win == 0:
            acc[...] = part
        else:
            acc[...] += part
    group = lax.broadcasted_iota(jnp.int32, (64, 128), 1) // 16
    for v in range(4):
        cols = slice(v * 128, v * 128 + 128)
        held = [
            jnp.concatenate(
                [acc[b * 64 + s * 8 : b * 64 + s * 8 + 8, cols] for b in range(8)], axis=0
            )
            for s in range(8)
        ]
        for bit in (4, 2, 1):
            low = (group & bit) == 0
            for s in range(8):
                if s & bit:
                    continue
                a, b = held[s], held[s + bit]
                held[s] = jnp.where(low, a, pltpu.roll(b, 16 * bit, axis=1))
                held[s + bit] = jnp.where(low, pltpu.roll(a, 128 - 16 * bit, axis=1), b)
        for g in range(0, 8, 2):
            row = (v * 8 + g) * 8
            for b in range(8):
                pair = jnp.concatenate(
                    [held[g][b * 8 : b * 8 + 8], held[g + 1][b * 8 : b * 8 + 8]], axis=0
                )
                out_ref[row : row + 16, b * 128 : b * 128 + 128] = pair.astype(jnp.bfloat16)


def cross_sums(src, rcv):
    return pl.pallas_call(
        cross_kernel,
        out_shape=jax.ShapeDtypeStruct((256, 1024), jnp.bfloat16),
        in_specs=[pl.BlockSpec(memory_space=pltpu.VMEM)] * 2,
        out_specs=pl.BlockSpec(memory_space=pltpu.VMEM),
        scratch_shapes=[pltpu.VMEM((512, 512), jnp.float32)],
        compiler_params=pltpu.CompilerParams(vmem_limit_bytes=VMEM),
    )(src, rcv)


def lag_kernel(cross_ref, high_ref, low_ref, out_ref):
    total = None
    for b in range(4):
        rows = cross_ref[:, b * 256 : b * 256 + 256]
        for table in (high_ref, low_ref):
            part = lax.dot_general(
                rows,
                table[b * 256 : b * 256 + 256, :],
                (((0,), (0,)), ((), ())),
                preferred_element_type=jnp.float32,
            )
            total = part if total is None else total + part
    out_ref[...] = total


def to_lags(cross, high, low):
    return pl.pallas_call(
        lag_kernel,
        out_shape=jax.ShapeDtypeStruct((256, LAGS), jnp.float32),
        grid=(4,),
        in_specs=[
            pl.BlockSpec((256, 1024), lambda i: (0, 0)),
            pl.BlockSpec((1024, 256), lambda i: (0, i)),
            pl.BlockSpec((1024, 256), lambda i: (0, i)),
        ],
        out_specs=pl.BlockSpec((256, 256), lambda i: (0, i)),
        compiler_params=pltpu.CompilerParams(vmem_limit_bytes=VMEM),
    )(cross, high, low)


def inverse_table():
    x, zh, core, win = np.meshgrid(
        np.arange(4), np.arange(4), np.arange(2), np.arange(8), indexing="ij"
    )
    place = (x * 128 + (win * 4 + zh) * 2 + core).reshape(-1)
    lag = np.arange(LAGS)
    rows = []
    for j in range(2):
        freq = place + 64 * j
        phase = (freq[:, None] * lag[None, :] % LAGS) * (2.0 * math.pi / LAGS)
        weight = np.where(freq == 0, 1.0, 2.0)[:, None] / math.sqrt(WINDOWS * LAGS)
        rows += [weight * np.cos(phase), -weight * np.sin(phase)]
    table = np.concatenate(rows, axis=0)
    high = jnp.asarray(table, jnp.float32).astype(jnp.bfloat16)
    low = (jnp.asarray(table, jnp.float32) - high.astype(jnp.float32)).astype(jnp.bfloat16)
    return high, low


def on_device(source_spectra, receiver_spectra, source_block, bad_channels):
    win_local, chans, _ = receiver_spectra.shape
    x, zh, core = (lax.axis_index(a) for a in ("x", "zh", "core"))
    holder = source_block[0]
    hx, hz, hc = holder // 8, (holder // 2) % 4, holder % 2

    channel_ids = ((x * 4 + zh) * 2 + core) * chans + jnp.arange(chans, dtype=jnp.int32)
    faulty = jnp.any(bad_channels[:, None] == channel_ids[None, :], axis=0)
    keep = jnp.where(faulty, 0.0, 1.0).astype(jnp.float32)[None, :, None]
    wide = receiver_spectra.astype(jnp.float32)
    r_re, r_im = whiten_parts(wide[..., :HALF], wide[..., HALF:])
    white = jnp.stack([r_re * keep, r_im * keep], axis=2).astype(jnp.bfloat16)
    blocks = white.reshape(win_local, chans, 2, 4, 2, 8, 8).transpose(5, 3, 6, 1, 4, 2, 0)
    blocks = blocks.reshape(256, chans, 128)
    rcv_at = lax.all_to_all(blocks, AXES, 0, 0, tiled=True).reshape(8, 512, 128)

    pieces = source_pieces(source_spectra, core, x)
    swap = [(0, 1), (1, 0)]
    up = [(i, (i + 1) % 4) for i in range(4)]
    down = [(i, (i + 3) % 4) for i in range(4)]
    half = {}
    for r in (2, 1, 3, 0):
        other = lax.ppermute(pieces[4 + r], "core", swap)
        half[r] = jnp.where(core == hc, pieces[r], other)
    mid = win_local // 2
    far_up = lax.ppermute(half[2][:mid], "x", up)
    far_down = lax.ppermute(half[2][mid:], "x", down)
    near_up = lax.ppermute(half[1], "x", up)
    near_down = lax.ppermute(half[3], "x", down)
    far_up = lax.ppermute(far_up, "x", up)
    far_down = lax.ppermute(far_down, "x", down)
    away = (x - hx) % 4
    far = jnp.concatenate([far_up, far_down], axis=0)
    quarter = jnp.where(
        away == 0,
        half[0],
        jnp.where(away == 1, near_up, jnp.where(away == 2, far, near_down)),
    )
    blocks = quarter.reshape(win_local, 8, 8, 2, 2, 64).transpose(5, 2, 1, 4, 3, 0)
    blocks = blocks.reshape(64, 64, 128)
    got = lax.all_to_all(blocks, ("y", "zl", "zh", "core"), 0, 0, tiled=True)
    got = lax.dynamic_index_in_dim(got.reshape(8, 4, 2, 64, 128), hz, 1, keepdims=False)
    src_at = got.reshape(8, 128, 128)

    sums = cross_sums(src_at, rcv_at)
    mine = lax.all_to_all(sums, ("x", "zh", "core", "y", "zl"), 0, 0, tiled=True)
    high, low = inverse_table()
    return to_lags(mine, high, low).reshape(16, 16, LAGS)


def solution(mesh):
    fine = Mesh(mesh.devices.reshape(SIZES), AXES)
    win, rcv = AXES[:2], AXES[2:]
    return jax.shard_map(
        on_device,
        mesh=fine,
        in_specs=(P(win, rcv, None), P(win, rcv, None), P(), P()),
        out_specs=P(win, rcv, None),
        check_vma=False,
    )
```

time: 653 us -> 207 us (0.32)
  waiting for transfers between devices: 480 us -> 74.6 us
  matrix products: 50.1 us -> 0 us
  starting transfers between devices: 0.04 us -> 34.7 us
  other arithmetic: 51.3 us -> 21.6 us
  blocking collectives: 0 us -> 27.4 us
  local copies, waits for them, and re-layouts: 56.2 us -> 33.6 us
  Pallas kernels: 0 us -> 14.5 us
  between operations: 14.2 us -> 0.89 us
    psum x1 -> x0, waiting for transfers between devices: 310 us -> none  [broadcast(): return lax.psum(kept, axis)]
    reduce_scatter x1 -> x0, waiting for transfers between devices: 170 us -> none  [on_device(): lax.psum_scatter(to_lags(cross, table), 'win', scatter_dimension=0, tiled...]
    dot_general x5 -> x0, matrix products: 50.1 us -> none  [the longest x1 32.1 us: to_lags(): jnp.dot(flat, table, precision=lax.Precision.HIGHEST, preferred_element_t...]
    ppermute x0 -> x10, waiting for transfers between devices: none -> 43.5 us  [the longest x1 30.1 us: on_device(): far_up = lax.ppermute(half[2][:mid], 'x', up)]
    all_to_all x0 -> x2, waiting for transfers between devices: none -> 31.1 us  [the longest x1 31.1 us: on_device(): rcv_at = lax.all_to_all(blocks, AXES, 0, 0, tiled=True).reshape(8, 512, 128)]
    all_to_all x0 -> x1, blocking collectives: none -> 27.4 us  [on_device(): lax.all_to_all(sums, ('x', 'zh', 'core', 'y', 'zl'), 0, 0, tiled=True)]
    slice x6 -> x1, local copies, waits for them, and re-layouts: 27.1 us -> 0.1 us  [on_device(): far_up = lax.ppermute(half[2][:mid], 'x', up)]
    all_to_all x0 -> x2, starting transfers between devices: none -> 24 us  [the longest x1 13 us: on_device(): rcv_at = lax.all_to_all(blocks, AXES, 0, 0, tiled=True).reshape(8, 512, 128)]
  transfers between devices with their start and end apart: 2 -> 12, of which waited for: 2 -> 4; matrix products, arithmetic and copies ran while one was open for 3% -> 18% of each run, Pallas kernels for 0% -> 0%
where the time goes in v1:
time: 207 us
  waiting for transfers between devices  74.6 us (36%)
  starting transfers between devices  34.7 us (17%)
  local copies, waits for them, and re-layouts  33.6 us (16%)
  blocking collectives  27.4 us (13%)
  other arithmetic  21.6 us (10%)
  Pallas kernels  14.5 us (7%)
    all_to_all x1, waiting for transfers between devices, on_device(): rcv_at = lax.all_to_all(blocks, AXES, 0, 0, tiled=True).reshape(8, 512, 128)  31.1 us
    ppermute x1, waiting for transfers between devices, on_device(): far_up = lax.ppermute(half[2][:mid], 'x', up)  30.1 us
    all_to_all x1, blocking collectives, on_device(): lax.all_to_all(sums, ('x', 'zh', 'core', 'y', 'zl'), 0, 0, tiled=True)  27.4 us
    all_to_all x1, starting transfers between devices, on_device(): rcv_at = lax.all_to_all(blocks, AXES, 0, 0, tiled=True).reshape(8, 512, 128)  13 us
    ppermute x1, waiting for transfers between devices, on_device(): far_up = lax.ppermute(far_up, 'x', up)  12 us
    all_to_all x1, starting transfers between devices, on_device(): got = lax.all_to_all(blocks, ('y', 'zl', 'zh', 'core'), 0, 0, tiled=True)  11 us
    unnamed x18, local copies, waits for them, and re-layouts  9.95 us
    pallas_call x1, Pallas kernels, source_pieces(): pl.pallas_call(source_kernel, out_shape=[piece] * 8, grid_spec=pltpu.Pref...  9.59 us
  transfers between devices with their start and end apart: 12, of which 4 were waited for; matrix products, arithmetic and copies ran while one was open for 18% of the time, Pallas kernels for 0%

profile of v1, /device:TPU:1, one launch (start us, length us, event | category | flops | bytes accessed | tf_op | source)
XLA Modules:
  0.0 207.3 jit_solution(9033056255252501828)
XLA Ops:
  0.0 0.1 pad_add_fusion.place
  0.1 9.6 %shard_map.64 = (bf16[32,64,256]{2,1,0:T(8,128)(2,1)S(1)}, bf16[32,64,256]{2,1,0:T(8,128)(2,1)S(1)}, bf16[32,64,256]{2,1,0:T(8,128)(2,1)S(1)}, bf16[32,64,256]{2...) custom-call(s32[2]{0:T(128)S(1)} %pad_add_fusion.place, ...), custom_call_target="tpu_custom_call" | custom-call | flops 40000000 | bytes 16777216 | tf_op jit(solution)/shard_map/pallas_call | solution.py:56
  9.7 1.0 copy-done.2
  10.6 3.2 %collective-permute-start.1 = (bf16[32,64,256]{2,1,0:T(8,128)(2,1)}, bf16[32,64,256]{2,1,0:T(8,128)(2,1)}, u32[]{:S(2)}, u32[]{:S(2)}) collective-permute-start(bf16[32,64,256]{2,1,0:T(8,128)(2,1)} %get-tuple-element.16), channel_id=1, source_target_pairs={{0,1},{1,0},{2,3},{3,2},{4,5},{5,4},{6,7},{7,6},{8,9},{9,8},{10,11... | collective-permute-start | bytes 3145736 | tf_op jit(solution)/shard_map/ppermute | solution.py:205
  13.9 0.0 collective-permute-start.3
  13.9 0.5 collective-permute-start.8
  14.4 0.0 collective-permute-start
  15.1 1.4 collective-permute-done.1
  16.5 2.3 %broadcast_select_fusion.2 = bf16[32,64,256]{2,1,0:T(8,128)(2,1)} fusion(bf16[32,64,256]{2,1,0:T(8,128)(2,1)S(1)} %get-tuple-element.15, bf16[32,64,256]{2,1,0:T(8,128)(2,1)} %collective-permute-done.1, pred[]{:T(512)S(6)} %eq.33), kind=kLoop, calls=%fused_computation.10 | loop fusion | flops 524288 | bytes 3145729 | tf_op jit(solution)/shard_map/jit(_where)/select_n | solution.py:206
  18.9 1.4 broadcast_select_fusion.1
  20.3 0.1 fusion.3
  20.4 0.8 collective-permute-start.4
  21.2 2.1 %collective-permute-start.6 = (bf16[16,64,256]{2,1,0:T(8,128)(2,1)S(1)}, bf16[16,64,256]{2,1,0:T(8,128)(2,1)}, u32[]{:S(2)}, u32[]{:S(2)}) collective-permute-start(bf16[16,64,256]{2,1,0:T(8,128)(2,1)S(1)} %get-tuple-element.24), channel_id=1, source_target_pairs={{0,24},{8,0},{16,8},{24,16},{1,25},{9,1},{17,9},{25,17},{2,26},{10... | collective-permute-start | bytes 1572872 | tf_op jit(solution)/shard_map/ppermute | solution.py:209
  23.2 1.3 broadcast_select_fusion
  24.6 1.5 collective-permute-start.9
  26.0 30.1 %collective-permute-done.4 = bf16[16,64,256]{2,1,0:T(8,128)(2,1)} collective-permute-done((bf16[16,64,256]{2,1,0:T(8,128)(2,1)S(1)}, bf16[16,64,256]{2,1,0:T(8,128)(2,1)}, u32[]{:S(2)}, u32[]{:S(2)}) %collective-permute-start.4) | collective-permute-done | bytes 524320 | tf_op jit(solution)/shard_map/ppermute | solution.py:208
  56.1 0.0 collective-permute-start.5
  56.1 0.0 collective-permute-done.6
  56.1 2.7 %collective-permute-start.7 = (bf16[16,64,256]{2,1,0:T(8,128)(2,1)}, bf16[16,64,256]{2,1,0:T(8,128)(2,1)}, u32[]{:S(2)}, u32[]{:S(2)}) collective-permute-start(bf16[16,64,256]{2,1,0:T(8,128)(2,1)} %collective-permute-done.6), channel_id=1, source_target_pairs={{0,24},{8,0},{16,8},{24,16},{1,25},{9,1},{17,9},{25,17},{2,26},{10... | collective-permute-start | bytes 1572872 | tf_op jit(solution)/shard_map/ppermute | solution.py:213
  58.8 12.0 %collective-permute-done.5 = bf16[16,64,256]{2,1,0:T(8,128)(2,1)} collective-permute-done((bf16[16,64,256]{2,1,0:T(8,128)(2,1)}, bf16[16,64,256]{2,1,0:T(8,128)(2,1)}, u32[]{:S(2)}, u32[]{:S(2)}) %collective-permute-start.5) | collective-permute-done | bytes 524320 | tf_op jit(solution)/shard_map/ppermute | solution.py:212
  70.8 1.8 fusion.1
  72.6 0.9 reshape.43
  73.4 0.0 copy-start.5
  73.4 3.8 %copy.25 = bf16[32,8,8,2,2,64]{5,0,3,4,1,2:T(8,128)(2,1)} copy(bf16[32,8,8,2,2,64]{5,4,3,2,1,0:T(2,128)(2,1)S(1)} %reshape.43) | data formatting | bytes 2097152 | tf_op jit(solution)/shard_map/reshape | solution.py:221
  77.2 3.4 %copy.26 = bf16[64,64,128]{2,1,0:T(8,128)(2,1)} copy(bf16[64,64,128]{0,2,1:T(8,128)(2,1)} %bitcast.26) | data formatting | bytes 2097152 | tf_op jit(solution)/shard_map/reshape | solution.py:222
  80.6 11.0 %all-to-all-start = ((bf16[64,64,128]{2,1,0:T(8,128)(2,1)}), bf16[64,64,128]{2,1,0:T(8,128)(2,1)S(1)}, u32[]{:S(2)}, u32[]{:S(2)}) async-start(bf16[64,64,128]{2,1,0:T(8,128)(2,1)} %copy.26), calls=%async_computation | async-start | bytes 2097152 | tf_op jit(solution)/shard_map/all_to_all | solution.py:223
  91.6 3.3 %copy.27 = bf16[32,16,1024]{0,2,1:T(8,128)(2,1)} copy(bf16[32,16,1024]{2,1,0:T(8,128)(2,1)S(1)} %copy-done.5) | data formatting | bytes 2097152 | tf_op args[1]
  94.9 6.3 %convert_element_type.14 = f32[32,16,1024]{0,2,1:T(8,128)} convert(bf16[32,16,1024]{0,2,1:T(8,128)(2,1)} %copy.27) | non-fusion elementwise | flops 524288 | bytes 3145728 | tf_op jit(solution)/shard_map/convert_element_type | solution.py:192
  101.2 0.2 compare_reduce_fusion
  101.4 4.3 %fusion.2 = f32[32,16]{0,1:T(8,128)S(1)} fusion(f32[32,16,1024]{0,2,1:T(8,128)} %convert_element_type.14), kind=kLoop, calls=%fused_computation.18 | loop fusion | flops 1048064 | bytes 2099200 | tf_op jit(solution)/shard_map/reduce_sum | solution.py:23
  105.7 1.5 copy-done.4
  107.2 1.8 multiply_convert_fusion.1
  109.1 0.9 maximum_bitcast_fusion
  110.0 6.3 %copy.28 = bf16[8,4,8,16,2,2,32]{6,5,4,3,2,1,0:T(2,128)(2,1)} copy(bf16[8,4,8,16,2,2,32]{6,2,0,4,1,3,5:T(8,128)(2,1)S(1)} %maximum_bitcast_fusion) | data formatting | bytes 2097152 | tf_op jit(solution)/shard_map/transpose | solution.py:195
  116.3 8.7 %reshape.47 = bf16[256,16,128]{2,1,0:T(8,128)(2,1)} reshape(bf16[8,4,8,16,2,2,32]{6,5,4,3,2,1,0:T(2,128)(2,1)} %copy.28) | data formatting | bytes 2097152 | tf_op jit(solution)/shard_map/reshape | solution.py:196
  125.0 13.0 %all-to-all-start.1 = ((bf16[256,16,128]{2,1,0:T(8,128)(2,1)}), bf16[256,16,128]{2,1,0:T(8,128)(2,1)S(1)}, u32[]{:S(2)}, u32[]{:S(2)}) async-start(bf16[256,16,128]{2,1,0:T(8,128)(2,1)} %reshape.47), calls=%async_computation.1 | async-start | bytes 2097152 | tf_op jit(solution)/shard_map/all_to_all | solution.py:197
  138.1 31.1 %all-to-all-done.1 = bf16[256,16,128]{2,1,0:T(8,128)(2,1)S(1)} async-done(((bf16[256,16,128]{2,1,0:T(8,128)(2,1)}), bf16[256,16,128]{2,1,0:T(8,128)(2,1)S(1)}, u32[]{:S(2)}, u32[]{:S(2)}) %all-to-all-start.1) | async-done | bytes 1048608 | tf_op jit(solution)/shard_map/all_to_all | solution.py:197
  169.2 1.6 shard_map.65
  170.9 0.5 broadcast.25
  171.4 1.0 reduce
  172.4 0.4 reshape.50
  172.8 27.4 %all_to_all.21 = bf16[256,2,512]{2,1,0:T(2,128)(2,1)S(1)} all-to-all(bf16[256,2,512]{2,1,0:T(2,128)(2,1)S(1)} %reshape.50), channel_id=1, replica_groups=mesh['y'=4,'zl'=2,'x'=4,'zh'=4,'core'=2] {'x','zh','core','y','zl'}, dimensions={0} | all-to-all | bytes 1048576 | tf_op jit(solution)/shard_map/all_to_all | solution.py:228
  200.2 0.4 reshape.51
  200.6 0.2 copy.32
  200.8 0.0 copy-start
  200.8 1.6 copy-done
  202.4 1.6 copy-done.1
  204.0 3.3 %shard_map.66 = f32[256,1024]{1,0:T(8,128)} custom-call(bf16[256,1024]{1,0:T(8,128)(2,1)S(1)} %bitcast.24, bf16[1024,1024]{1,0:T(8,128)(2,1)S(1)} %copy-done.1, bf16[1024,1024]{1,0:T(8,128)(2,1)S(1)} %copy-done), custom_call_target="tpu_custom_call" | custom-call | tf_op jit(solution)/shard_map/pallas_call | solution.py:151
  (20 shorter events, 0.1 us)
Async XLA Ops:
  9.7 1.0 copy-start.2
  10.6 5.9 %collective-permute-start.1 = (bf16[32,64,256]{2,1,0:T(8,128)(2,1)}, bf16[32,64,256]{2,1,0:T(8,128)(2,1)}, u32[]{:S(2)}, u32[]{:S(2)}) collective-permute-start(bf16[32,64,256]{2,1,0:T(8,128)(2,1)} %get-tuple-element.16), channel_id=1, source_target_pairs={{0,1},{1,0},{2,3},{3,2},{4,5},{5,4},{6,7},{7,6},{8,9},{9,8},{10,11... | collective-permute-start | bytes 3145736 | tf_op jit(solution)/shard_map/ppermute | solution.py:205
  13.9 5.0 %collective-permute-start.3 = (bf16[32,64,256]{2,1,0:T(8,128)(2,1)}, bf16[32,64,256]{2,1,0:T(8,128)(2,1)}, u32[]{:S(2)}, u32[]{:S(2)}) collective-permute-start(bf16[32,64,256]{2,1,0:T(8,128)(2,1)} %get-tuple-element.18), channel_id=1, source_target_pairs={{0,1},{1,0},{2,3},{3,2},{4,5},{5,4},{6,7},{7,6},{8,9},{9,8},{10,11... | collective-permute-start | bytes 3145736 | tf_op jit(solution)/shard_map/ppermute | solution.py:205
  13.9 9.4 %collective-permute-start.8 = (bf16[32,64,256]{2,1,0:T(8,128)(2,1)}, bf16[32,64,256]{2,1,0:T(8,128)(2,1)}, u32[]{:S(2)}, u32[]{:S(2)}) collective-permute-start(bf16[32,64,256]{2,1,0:T(8,128)(2,1)} %get-tuple-element.20), channel_id=1, source_target_pairs={{0,1},{1,0},{2,3},{3,2},{4,5},{5,4},{6,7},{7,6},{8,9},{9,8},{10,11... | collective-permute-start | bytes 3145736 | tf_op jit(solution)/shard_map/ppermute | solution.py:205
  14.4 44.4 %collective-permute-start = (bf16[32,64,256]{2,1,0:T(8,128)(2,1)}, bf16[32,64,256]{2,1,0:T(8,128)(2,1)}, u32[]{:S(2)}, u32[]{:S(2)}) collective-permute-start(bf16[32,64,256]{2,1,0:T(8,128)(2,1)} %get-tuple-element.14), channel_id=1, source_target_pairs={{0,1},{1,0},{2,3},{3,2},{4,5},{5,4},{6,7},{7,6},{8,9},{9,8},{10,11... | collective-permute-start | bytes 3145736 | tf_op jit(solution)/shard_map/ppermute | solution.py:205
  18.9 39.9 %collective-permute-start.2 = (bf16[32,64,256]{2,1,0:T(8,128)(2,1)}, bf16[32,64,256]{2,1,0:T(8,128)(2,1)}, u32[]{:S(2)}, u32[]{:S(2)}) collective-permute-start(bf16[32,64,256]{2,1,0:T(8,128)(2,1)} %broadcast_select_fusion.2), channel_id=1, source_target_pairs={{0,8},{8,16},{16,24},{24,0},{1,9},{9,17},{17,25},{25,1},{2,10},{10... | collective-permute-start | bytes 3145736 | tf_op jit(solution)/shard_map/ppermute | solution.py:210
  18.9 51.9 %copy-start.3 = (bf16[32,64,256]{2,1,0:T(8,128)(2,1)S(1)}, bf16[32,64,256]{2,1,0:T(8,128)(2,1)}, u32[]{:S(2)}) copy-start(bf16[32,64,256]{2,1,0:T(8,128)(2,1)} %copy-done.2) | copy-start | bytes 3145732
  20.4 35.7 %collective-permute-start.4 = (bf16[16,64,256]{2,1,0:T(8,128)(2,1)S(1)}, bf16[16,64,256]{2,1,0:T(8,128)(2,1)}, u32[]{:S(2)}, u32[]{:S(2)}) collective-permute-start(bf16[16,64,256]{2,1,0:T(8,128)(2,1)S(1)} %get-tuple-element.23), channel_id=1, source_target_pairs={{0,8},{8,16},{16,24},{24,0},{1,9},{9,17},{17,25},{25,1},{2,10},{10... | collective-permute-start | bytes 1572872 | tf_op jit(solution)/shard_map/ppermute | solution.py:208
  21.2 35.0 %collective-permute-start.6 = (bf16[16,64,256]{2,1,0:T(8,128)(2,1)S(1)}, bf16[16,64,256]{2,1,0:T(8,128)(2,1)}, u32[]{:S(2)}, u32[]{:S(2)}) collective-permute-start(bf16[16,64,256]{2,1,0:T(8,128)(2,1)S(1)} %get-tuple-element.24), channel_id=1, source_target_pairs={{0,24},{8,0},{16,8},{24,16},{1,25},{9,1},{17,9},{25,17},{2,26},{10... | collective-permute-start | bytes 1572872 | tf_op jit(solution)/shard_map/ppermute | solution.py:209
  24.6 46.2 %collective-permute-start.9 = (bf16[32,64,256]{2,1,0:T(8,128)(2,1)S(1)}, bf16[32,64,256]{2,1,0:T(8,128)(2,1)S(1)}, u32[]{:S(2)}, u32[]{:S(2)}) collective-permute-start(bf16[32,64,256]{2,1,0:T(8,128)(2,1)S(1)} %broadcast_select_fusion), channel_id=1, source_target_pairs={{0,24},{8,0},{16,8},{24,16},{1,25},{9,1},{17,9},{25,17},{2,26},{10... | collective-permute-start | bytes 3145736 | tf_op jit(solution)/shard_map/ppermute | solution.py:211
  56.1 14.6 %collective-permute-start.5 = (bf16[16,64,256]{2,1,0:T(8,128)(2,1)}, bf16[16,64,256]{2,1,0:T(8,128)(2,1)}, u32[]{:S(2)}, u32[]{:S(2)}) collective-permute-start(bf16[16,64,256]{2,1,0:T(8,128)(2,1)} %collective-permute-done.4), channel_id=1, source_target_pairs={{0,8},{8,16},{16,24},{24,0},{1,9},{9,17},{17,25},{25,1},{2,10},{10... | collective-permute-start | bytes 1572872 | tf_op jit(solution)/shard_map/ppermute | solution.py:212
  56.1 14.6 %collective-permute-start.7 = (bf16[16,64,256]{2,1,0:T(8,128)(2,1)}, bf16[16,64,256]{2,1,0:T(8,128)(2,1)}, u32[]{:S(2)}, u32[]{:S(2)}) collective-permute-start(bf16[16,64,256]{2,1,0:T(8,128)(2,1)} %collective-permute-done.6), channel_id=1, source_target_pairs={{0,24},{8,0},{16,8},{24,16},{1,25},{9,1},{17,9},{25,17},{2,26},{10... | collective-permute-start | bytes 1572872 | tf_op jit(solution)/shard_map/ppermute | solution.py:213
  73.4 18.2 %copy-start.5 = (bf16[32,16,1024]{2,1,0:T(8,128)(2,1)S(1)}, bf16[32,16,1024]{2,1,0:T(8,128)(2,1)}, u32[]{:S(2)}) copy-start(bf16[32,16,1024]{2,1,0:T(8,128)(2,1)} %param.7) | copy-start | bytes 3145732
  80.6 44.4 %all-to-all-start = ((bf16[64,64,128]{2,1,0:T(8,128)(2,1)}), bf16[64,64,128]{2,1,0:T(8,128)(2,1)S(1)}, u32[]{:S(2)}, u32[]{:S(2)}) async-start(bf16[64,64,128]{2,1,0:T(8,128)(2,1)} %copy.26), calls=%async_computation | async-start | bytes 2097152 | tf_op jit(solution)/shard_map/all_to_all | solution.py:223
  94.9 6.3 %copy-start.6 = (s32[64]{0:T(128)S(1)}, s32[64]{0:T(128)}, u32[]{:S(2)}) copy-start(s32[64]{0:T(128)} %param.9) | copy-start | bytes 772
  101.4 5.8 %copy-start.4 = (f32[32,16,1024]{0,2,1:T(8,128)S(1)}, f32[32,16,1024]{0,2,1:T(8,128)}, u32[]{:S(2)}) copy-start(f32[32,16,1024]{0,2,1:T(8,128)} %convert_element_type.14) | copy-start | bytes 6291460
  125.0 44.2 %all-to-all-start.1 = ((bf16[256,16,128]{2,1,0:T(8,128)(2,1)}), bf16[256,16,128]{2,1,0:T(8,128)(2,1)S(1)}, u32[]{:S(2)}, u32[]{:S(2)}) async-start(bf16[256,16,128]{2,1,0:T(8,128)(2,1)} %reshape.47), calls=%async_computation.1 | async-start | bytes 2097152 | tf_op jit(solution)/shard_map/all_to_all | solution.py:197
  200.8 1.6 copy-start
  202.4 1.6 copy-start.1
